TPU v7x, 32 devices: a whole 2x2x4 slice. The times are simulated.
32 devices in a mesh: groups: 2 (over y), chan: 16 (over z, x, core).
Axes of the slice: x: 2, y: 2, z: 4, core: 2. Of those that a mesh axis runs over, the one named last changes fastest.
Arguments:
- eta: bfloat16 [16384, 512], P(('groups', 'chan')), parts along dimension 0, as said below
- ham: bfloat16 [16384, 512], P(('groups', 'chan')), parts along dimension 0, as said below
- pp_occ: int32 [32, 2, 512], P(('groups', 'chan')), parts along dimension 0, may hold values 0 or 1
- ph_occ: int32 [32, 2, 512], P(('groups', 'chan')), parts along dimension 0, may hold values 0 or 1
- ph_src: int32 [32, 16, 8], P(('groups', 'chan')), parts along dimension 0, may hold values from 0 to 255, as said below
- coef6j: float32 [32, 16, 8], P(('groups', 'chan')), parts along dimension 0, may hold values from -1 to 1
Outputs:
- flow: float32 [16384, 512], P(('groups', 'chan')), parts along dimension 0
There are 2 independent parts, one for each index of `groups`. A program takes and returns all parts, laid end to end along the dimension named above; each array names one. Nothing has to cross between parts.
Inputs may be any that keep to these rules, and one draw needn't show every extreme that they name: eta is antisymmetric and ham symmetric within each channel's 512 x 512 block. ham is symmetric within each channel's block. ph_src names pp block g = c * 16 + b; within one ph channel no block is named twice, and every pp channel that it names gives exactly 8 of its blocks.
All inputs are finite; a program needn't handle non-finite values. No bound on the sum of `pp_occ` or of `ph_occ` on one device may be relied on, other than what follows from the above.
Results may differ from a plain program's by a relative error of at most 0.0048.
Values may be sent and summed in bfloat16 or wider, within the bound.
A program may use at most 128 MiB of HBM per device.

v0:
```python
import jax
import jax.numpy as jnp
from jax import lax
from jax.sharding import PartitionSpec as P

B = 128
NBR = 4
K = 8
NBLK = 16


def on_device(eta, ham, pp_occ, ph_occ, ph_src, coef6j):
    chan_count = lax.axis_size("chan")
    chan_order = eta.shape[0]
    tile_size = B
    row_tiles = NBR
    tile_count = NBLK
    term_count = tile_count * K
    capacity = max(2, term_count // chan_count)

    def split_tiles(matrix):
        return (
            matrix.reshape(row_tiles, tile_size, row_tiles, tile_size)
            .transpose(0, 2, 1, 3)
            .reshape(tile_count, tile_size, tile_size)
        )

    def join_tiles(tiles):
        return (
            tiles.reshape(row_tiles, row_tiles, tile_size, tile_size)
            .transpose(0, 2, 1, 3)
            .reshape(chan_order, chan_order)
        )

    ref_list = ph_src.reshape(term_count)
    source = ref_list // tile_count
    within = ref_list % tile_count
    lane_ids = jnp.arange(chan_count, dtype=jnp.int32)
    hit_table = (source[:, None] == lane_ids[None, :]).astype(jnp.int32)
    slot_of = jnp.sum(jnp.cumsum(hit_table, axis=0) * hit_table, axis=1) - 1
    place_at = source * capacity + slot_of
    wanted = (
        jnp.full((chan_count * capacity,), -1, jnp.int32)
        .at[place_at]
        .set(within)
        .reshape(chan_count, capacity)
    )
    asked_for = lax.all_to_all(wanted, "chan", split_axis=0, concat_axis=0, tiled=True)
    weights = coef6j.reshape(tile_count, K)
    live = (asked_for >= 0)[:, :, None, None]
    safe_ids = jnp.maximum(asked_for, 0)

    def mix_terms(picked):
        shaped = picked.reshape(tile_count, K, tile_size, tile_size)
        total = jnp.zeros((tile_count, tile_size, tile_size), jnp.float32)
        for term in range(K):
            total = total + shaped[:, term].astype(jnp.float32) * weights[:, term][:, None, None]
        return join_tiles(total.astype(jnp.bfloat16))

    eta_tiles = split_tiles(eta)
    ham_tiles = split_tiles(ham)
    pair_blocks = jnp.stack([eta_tiles, ham_tiles], axis=1)
    outgoing = jnp.where(live[:, :, None], pair_blocks[safe_ids], jnp.zeros((), jnp.bfloat16))
    incoming = lax.all_to_all(outgoing, "chan", split_axis=0, concat_axis=0, tiled=True)
    picked = incoming.reshape(chan_count * capacity, 2, tile_size, tile_size)[place_at]
    ph_eta = mix_terms(picked[:, 0])
    ph_ham = mix_terms(picked[:, 1])
    occ_ph = (ph_occ[0, 0] - ph_occ[0, 1]).astype(jnp.bfloat16)
    z_matrix = jnp.dot(
        ph_eta * occ_ph[None, :], ph_ham, preferred_element_type=jnp.float32
    ) - jnp.dot(ph_ham * occ_ph[None, :], ph_eta, preferred_element_type=jnp.float32)
    back_terms = (
        (split_tiles(z_matrix)[:, None] * weights[:, :, None, None])
        .astype(jnp.bfloat16)
        .reshape(term_count, tile_size, tile_size)
    )
    outgoing_back = (
        jnp.zeros((chan_count * capacity, tile_size, tile_size), jnp.bfloat16)
        .at[place_at]
        .set(back_terms)
        .reshape(chan_count, capacity, tile_size, tile_size)
    )
    returned = lax.all_to_all(outgoing_back, "chan", split_axis=0, concat_axis=0, tiled=True)
    tile_ids = jnp.arange(tile_count, dtype=jnp.int32)
    selector = (asked_for.reshape(chan_count * capacity)[None, :] == tile_ids[:, None]).astype(
        jnp.bfloat16
    )
    ph_term = jnp.dot(
        selector,
        returned.reshape(chan_count * capacity, tile_size * tile_size),
        preferred_element_type=jnp.float32,
    ).reshape(tile_count, tile_size, tile_size)
    occ_pp = (1 - pp_occ[0, 0] - pp_occ[0, 1]).astype(jnp.bfloat16)
    ladder = jnp.dot(eta * occ_pp[None, :], ham, preferred_element_type=jnp.float32) - jnp.dot(
        ham * occ_pp[None, :], eta, preferred_element_type=jnp.float32
    )
    return ladder + join_tiles(ph_term)


def solution(mesh):
    return jax.shard_map(
        on_device,
        mesh=mesh,
        in_specs=(
            P(("groups", "chan"), None),
            P(("groups", "chan"), None),
            P(("groups", "chan"), None, None),
            P(("groups", "chan"), None, None),
            P(("groups", "chan"), None, None),
            P(("groups", "chan"), None, None),
        ),
        out_specs=P(("groups", "chan"), None),
        check_vma=False,
    )
```

profile of v0, /device:TPU:11, one launch (start us, length us, event | category | flops | bytes accessed | tf_op | source)
XLA Modules:
  0.0 378.9 jit_solution(9546261654395165108)
XLA Ops:
  0.0 0.8 copy.58
  1.4 1.0 scatter_custom_fusion
  2.4 0.7 all_to_all.12
  3.1 6.6 %all-to-all-start = ((s32[16,1,8]{2,1,0:T(1,128)}), s32[16,1,8]{2,1,0:T(1,128)S(1)}, u32[]{:S(2)}, u32[]{:S(2)}) async-start(s32[16,1,8]{2,1,0:T(1,128)} %bitcast.2), calls=%async_computation | async-start | bytes 16384 | tf_op jit(solution)/shard_map/all_to_all | solution.py:48
  9.6 1.2 reshape.319
  10.9 1.2 reshape.320
  12.3 1.1 all-to-all-done
  13.7 6.6 %gather_fusion = bf16[128,2,128,128]{3,2,1,0:T(8,128)(2,1)} fusion(bf16[16,2,128,128]{3,2,0,1:T(8,128)(2,1)S(1)} %pad_maximum_fusion, s32[1024]{0:T(1024)S(1)} %pad_clamp_fusion.1), kind=kCustom, calls=%fused_computation | custom fusion | bytes 16777728 | tf_op jit(solution)/shard_map/gather | solution.py:63
  20.3 7.2 %broadcast_select_fusion = bf16[16,8,2,128,128]{4,3,2,1,0:T(8,128)(2,1)} fusion(bf16[16,8,2,128,128]{4,3,2,1,0:T(8,128)(2,1)} %bitcast.176, pred[16,8]{1,0:T(8,128)(4,1)S(1)} %copy.62), kind=kLoop, calls=%fused_computation.6 | loop fusion | flops 4194304 | bytes 16777344 | tf_op jit(solution)/shard_map/jit(_where)/select_n | solution.py:63
  27.5 7.3 %all-to-all-start.1 = ((bf16[16,8,2,128,128]{4,3,2,1,0:T(8,128)(2,1)}), bf16[16,8,2,128,128]{4,3,2,1,0:T(8,128)(2,1)}, u32[]{:S(2)}, u32[]{:S(2)}) async-start(bf16[16,8,2,128,128]{4,3,2,1,0:T(8,128)(2,1)} %broadcast_select_fusion), calls=%async_computation.1 | async-start | bytes 16777216 | tf_op jit(solution)/shard_map/all_to_all | solution.py:64
  35.7 181.5 %all-to-all-done.1 = bf16[16,8,2,128,128]{4,3,2,1,0:T(8,128)(2,1)} async-done(((bf16[16,8,2,128,128]{4,3,2,1,0:T(8,128)(2,1)}), bf16[16,8,2,128,128]{4,3,2,1,0:T(8,128)(2,1)}, u32[]{:S(2)}, u32[]{:S(2)}) %all-to-all-start.1) | async-done | bytes 8388640 | tf_op jit(solution)/shard_map/all_to_all | solution.py:64
  217.2 9.9 %gather_fusion.1 = bf16[128,2,128,128]{3,2,1,0:T(8,128)(2,1)} fusion(bf16[128,2,128,128]{3,2,1,0:T(8,128)(2,1)} %bitcast.11, s32[1024]{0:T(1024)S(1)} %pad_clamp_fusion), kind=kCustom, calls=%fused_computation.1 | custom fusion | bytes 16777728 | tf_op jit(solution)/shard_map/gather | solution.py:65
  227.2 4.0 %fusion.45 = (bf16[128,1,128,128]{3,2,1,0:T(8,128)(2,1)S(1)}, bf16[128,1,128,128]{3,2,1,0:T(8,128)(2,1)S(1)}) fusion(bf16[128,2,128,128]{3,2,1,0:T(8,128)(2,1)} %gather_fusion.1), kind=kLoop, calls=%fused_computation.99 | loop fusion | bytes 16777216 | tf_op jit(solution)/shard_map/slice | solution.py:66
  231.2 0.5 fusion.46
  231.7 1.0 broadcast_multiply_fusion.1
  232.7 0.4 copy.67
  233.1 0.5 fusion.47
  233.7 1.0 broadcast_multiply_fusion
  235.9 0.4 fusion.22
  236.4 0.4 convolution_subtract_fusion
  237.3 2.7 fusion
  240.0 3.0 broadcast_in_dim.17
  243.0 19.4 %scatter_fusion = bf16[128,128,128]{2,1,0:T(8,128)(2,1)} fusion(bf16[128,128,128]{2,1,0:T(8,128)(2,1)} %broadcast_in_dim.17, s32[128]{0:T(128)S(1)} %fusion.40, bf16[128,128,128]{2,1,0:T(8,128)(2,1)} %fusion), kind=kCustom, calls=%fused_computation.3 | custom fusion | bytes 12583424 | tf_op jit(solution)/shard_map/scatter | solution.py:80
  262.4 5.1 %all-to-all-start.2 = ((bf16[16,8,128,128]{3,2,1,0:T(8,128)(2,1)}), bf16[16,8,128,128]{3,2,1,0:T(8,128)(2,1)}, u32[]{:S(2)}, u32[]{:S(2)}) async-start(bf16[16,8,128,128]{3,2,1,0:T(8,128)(2,1)} %bitcast.175), calls=%async_computation.2 | async-start | bytes 8388608 | tf_op jit(solution)/shard_map/all_to_all | solution.py:83
  267.5 0.4 fusion.28
  268.0 0.5 broadcast.245
  268.5 0.7 reduce.39
  269.2 90.7 %all-to-all-done.2 = bf16[16,8,128,128]{3,2,1,0:T(8,128)(2,1)} async-done(((bf16[16,8,128,128]{3,2,1,0:T(8,128)(2,1)}), bf16[16,8,128,128]{3,2,1,0:T(8,128)(2,1)}, u32[]{:S(2)}, u32[]{:S(2)}) %all-to-all-start.2) | async-done | bytes 4194336 | tf_op jit(solution)/shard_map/all_to_all | solution.py:83
  359.9 7.7 %copy.99 = bf16[16,8,128,128]{3,1,2,0:T(8,128)(2,1)} copy(bf16[16,8,128,128]{3,2,1,0:T(8,128)(2,1)} %all-to-all-done.2) | data formatting | bytes 8388608
  367.6 6.4 %copy.73 = bf16[16384,128]{1,0:T(8,128)(2,1)} copy(bf16[16384,128]{0,1:T(8,128)(2,1)} %bitcast.178) | data formatting | bytes 8388608 | tf_op jit(solution)/shard_map/dot_general | solution.py:88
  374.0 3.4 fusion.35
  377.4 1.4 fusion.1
  (48 shorter events, 4.0 us)
Async XLA Ops:
  3.1 10.3 %all-to-all-start = ((s32[16,1,8]{2,1,0:T(1,128)}), s32[16,1,8]{2,1,0:T(1,128)S(1)}, u32[]{:S(2)}, u32[]{:S(2)}) async-start(s32[16,1,8]{2,1,0:T(1,128)} %bitcast.2), calls=%async_computation | async-start | bytes 16384 | tf_op jit(solution)/shard_map/all_to_all | solution.py:48
  27.5 7.3 %copy-start.2 = (f32[1,16,8]{1,2,0:T(8,128)S(1)}, f32[1,16,8]{1,2,0:T(8,128)}, u32[]{:S(2)}) copy-start(f32[1,16,8]{1,2,0:T(8,128)} %param.11) | copy-start | bytes 1540
  27.5 8.2 %copy-start.3 = (s32[1,2,512]{2,1,0:T(2,128)S(1)}, s32[1,2,512]{2,1,0:T(2,128)}, u32[]{:S(2)}) copy-start(s32[1,2,512]{2,1,0:T(2,128)} %param.9) | copy-start | bytes 12292
  27.5 189.7 %all-to-all-start.1 = ((bf16[16,8,2,128,128]{4,3,2,1,0:T(8,128)(2,1)}), bf16[16,8,2,128,128]{4,3,2,1,0:T(8,128)(2,1)}, u32[]{:S(2)}, u32[]{:S(2)}) async-start(bf16[16,8,2,128,128]{4,3,2,1,0:T(8,128)(2,1)} %broadcast_select_fusion), calls=%async_computation.1 | async-start | bytes 16777216 | tf_op jit(solution)/shard_map/all_to_all | solution.py:64
  262.4 5.1 %copy-start.4 = (s32[1,2,512]{2,1,0:T(2,128)S(1)}, s32[1,2,512]{2,1,0:T(2,128)}, u32[]{:S(2)}) copy-start(s32[1,2,512]{2,1,0:T(2,128)} %param.8) | copy-start | bytes 12292
  262.4 5.1 %copy-start = (bf16[512,512]{1,0:T(8,128)(2,1)S(1)}, bf16[512,512]{1,0:T(8,128)(2,1)}, u32[]{:S(2)}) copy-start(bf16[512,512]{1,0:T(8,128)(2,1)} %param.7) | copy-start | bytes 1572868
  262.4 5.1 %copy-start.1 = (bf16[512,512]{1,0:T(8,128)(2,1)S(1)}, bf16[512,512]{1,0:T(8,128)(2,1)}, u32[]{:S(2)}) copy-start(bf16[512,512]{1,0:T(8,128)(2,1)} %param.6) | copy-start | bytes 1572868
  262.4 97.5 %all-to-all-start.2 = ((bf16[16,8,128,128]{3,2,1,0:T(8,128)(2,1)}), bf16[16,8,128,128]{3,2,1,0:T(8,128)(2,1)}, u32[]{:S(2)}, u32[]{:S(2)}) async-start(bf16[16,8,128,128]{3,2,1,0:T(8,128)(2,1)} %bitcast.175), calls=%async_computation.2 | async-start | bytes 8388608 | tf_op jit(solution)/shard_map/all_to_all | solution.py:83
where the time goes:
time: 380 us; the launch traced here: 379 us
  waiting for transfers between devices  273 us (72%)
  local copies, waits for them, and re-layouts  67.1 us (18%)
  starting transfers between devices  19 us (5%)
  other arithmetic  13.2 us (3%)
  matrix products  6.17 us (2%)
    all_to_all x1, waiting for transfers between devices, on_device(): lax.all_to_all(outgoing, 'chan', split_axis=0, concat_axis=0, tiled=True)  181 us
    all_to_all x1, waiting for transfers between devices, on_device(): lax.all_to_all(outgoing_back, 'chan', split_axis=0, concat_axis=0, tiled=...  90.7 us
    scatter x1, local copies, waits for them, and re-layouts, on_device(): outgoing_back = jnp.zeros((chan_count * capacity, tile_size, tile_size),...  19.4 us
    gather x1, local copies, waits for them, and re-layouts, on_device(): incoming.reshape(chan_count * capacity, 2, tile_size, tile_size)[place_at]  9.95 us
    unnamed x13, local copies, waits for them, and re-layouts  8.55 us
  transfers between devices with their start and end apart: 3, of which 3 were waited for; matrix products, arithmetic and copies ran while one was open for 1% of the time, Pallas kernels for 0%

commit v1 on v0

--- a/solution.py
+++ b/solution.py
@@ -1,15 +1,22 @@
+import functools
+
 import jax
 import jax.numpy as jnp
 from jax import lax
+from jax.experimental import pallas as pl
+from jax.experimental.pallas import tpu as pltpu
 from jax.sharding import PartitionSpec as P
 
 B = 128
 NBR = 4
 K = 8
 NBLK = 16
-
-
-def on_device(eta, ham, pp_occ, ph_occ, ph_src, coef6j):
+TERMS = NBLK * K
+MESH = pl.DeviceIdType.MESH
+LIMIT = 48 * 1024 * 1024
+
+
+def exchange_plan(eta, ham, pp_occ, ph_occ, ph_src, coef6j):
     chan_count = lax.axis_size("chan")
     chan_order = eta.shape[0]
     tile_size = B
@@ -97,9 +104,298 @@
     return ladder + join_tiles(ph_term)
 
 
+LEVELS = 4
+
+
+def gather_kernel(eta_ref, ham_ref, occ_ref, all_ref, ladder_ref, mine, send_z, send_x, send_c, recv, local):
+    group = lax.axis_index("groups")
+    me = lax.axis_index("chan")
+    level = me // 4
+    side = (me // 2) % 2
+    core = me % 2
+
+    def chan_at(lvl, sd, cr):
+        return (lvl * 2 + sd) * 2 + cr
+
+    up = chan_at(level + 1, side, core)
+    down = chan_at(level - 1, side, core)
+    across = chan_at(level, 1 - side, core)
+    twin = chan_at(level, side, 1 - core)
+    has_up = level < LEVELS - 1
+    has_down = level > 0
+
+    barrier = pltpu.get_barrier_semaphore()
+
+    def greet(target):
+        pl.semaphore_signal(barrier, inc=1, device_id=(group, target), device_id_type=MESH)
+
+    greet(across)
+    greet(twin)
+
+    @pl.when(has_up)
+    def _():
+        greet(up)
+
+    @pl.when(has_down)
+    def _():
+        greet(down)
+
+    rows = lax.broadcasted_iota(jnp.int32, (B, B), 0)
+    cols = lax.broadcasted_iota(jnp.int32, (B, B), 1)
+    for r in range(NBR):
+        for s in range(NBR):
+            here = (pl.ds(r * B, B), pl.ds(s * B, B))
+            if r < s:
+                mine[r * NBR + s] = eta_ref[here]
+            elif r > s:
+                mine[r * NBR + s] = ham_ref[here]
+            else:
+                mine[r * NBR + s] = jnp.where(rows < cols, eta_ref[here], ham_ref[here])
+
+    pl.semaphore_wait(barrier, 2 + has_up.astype(jnp.int32) + has_down.astype(jnp.int32))
+
+    def remote(src, own, sem, target):
+        return pltpu.make_async_remote_copy(
+            src_ref=mine if own else all_ref.at[src],
+            dst_ref=all_ref.at[src],
+            send_sem=sem,
+            recv_sem=recv.at[src],
+            device_id=(group, target),
+            device_id_type=MESH,
+        )
+
+    def arrived(src):
+        remote(src, True, send_c.at[0], twin).wait_recv()
+
+    def column_step(step, action):
+        for way in (0, 1):
+            if step == 0 and way == 1:
+                continue
+            lvl = level - step if way == 0 else level + step
+            inside = lvl >= 0 if way == 0 else lvl < LEVELS
+
+            @pl.when(inside)
+            def _():
+                action(step, way, lvl)
+
+    def handle(step, way, lvl):
+        src = chan_at(lvl, side, core)
+        own = step == 0
+        if not own:
+            arrived(src)
+        if own or way == 0:
+            @pl.when(has_up)
+            def _():
+                remote(src, own, send_z.at[0, step], up).start()
+        if own or way == 1:
+            @pl.when(has_down)
+            def _():
+                remote(src, own, send_z.at[1, step], down).start()
+        remote(src, own, send_x.at[way, step], across).start()
+        remote(src, own, send_c.at[way * LEVELS + step], twin).start()
+
+    def handle_across(step, way, lvl):
+        src = chan_at(lvl, 1 - side, core)
+        arrived(src)
+        remote(src, False, send_c.at[2 * LEVELS + way * LEVELS + step], twin).start()
+
+    column_step(0, handle)
+    keep = pltpu.make_async_copy(mine, all_ref.at[me], local)
+    keep.start()
+    occ = occ_ref[...]
+    for r in range(NBR):
+        band = pl.ds(r * B, B)
+        ladder_ref[band, :] = jnp.dot(
+            eta_ref[band, :] * occ, ham_ref[...], preferred_element_type=jnp.float32
+        ) - jnp.dot(ham_ref[band, :] * occ, eta_ref[...], preferred_element_type=jnp.float32)
+    for step in range(1, LEVELS):
+        column_step(step, handle)
+        column_step(step - 1, handle_across)
+    column_step(LEVELS - 1, handle_across)
+
+    def finish(step, way, lvl):
+        own = step == 0
+        src = chan_at(lvl, side, core)
+        if own or way == 0:
+            @pl.when(has_up)
+            def _():
+                remote(src, own, send_z.at[0, step], up).wait_send()
+        if own or way == 1:
+            @pl.when(has_down)
+            def _():
+                remote(src, own, send_z.at[1, step], down).wait_send()
+        remote(src, own, send_x.at[way, step], across).wait_send()
+        remote(src, own, send_c.at[way * LEVELS + step], twin).wait_send()
+        other = chan_at(lvl, 1 - side, core)
+        remote(other, False, send_c.at[2 * LEVELS + way * LEVELS + step], twin).wait_send()
+
+    def finish_twin(step, way, lvl):
+        arrived(chan_at(lvl, side, 1 - core))
+        arrived(chan_at(lvl, 1 - side, 1 - core))
+
+    for step in range(LEVELS):
+        column_step(step, finish_twin)
+        column_step(step, finish)
+    keep.wait()
+
+
+def gather_packed(eta, ham, occ, chan_count):
+    order = eta.shape[0]
+    vmem = pl.BlockSpec(memory_space=pltpu.VMEM)
+    return pl.pallas_call(
+        gather_kernel,
+        out_shape=(
+            jax.ShapeDtypeStruct((chan_count, NBLK, B, B), jnp.bfloat16),
+            jax.ShapeDtypeStruct((order, order), jnp.float32),
+        ),
+        in_specs=[vmem, vmem, vmem],
+        out_specs=(pl.BlockSpec(memory_space=pl.ANY), vmem),
+        scratch_shapes=[
+            pltpu.VMEM((NBLK, B, B), jnp.bfloat16),
+            pltpu.SemaphoreType.DMA((2, LEVELS)),
+            pltpu.SemaphoreType.DMA((2, LEVELS)),
+            pltpu.SemaphoreType.DMA((4 * LEVELS,)),
+            pltpu.SemaphoreType.DMA((chan_count,)),
+            pltpu.SemaphoreType.DMA,
+        ],
+        compiler_params=pltpu.CompilerParams(
+            collective_id=0, has_side_effects=True, vmem_limit_bytes=LIMIT
+        ),
+    )(eta, ham, occ)
+
+
+def recouple_kernel(refs, coef, picks, packed, occ, own_ref, twin_ref, eta_full, ham_full, mix_eta, mix_ham, z_tiles, sums):
+    chan_count = packed.shape[0]
+    local_count = occ.shape[0]
+    rows = lax.broadcasted_iota(jnp.int32, (B, B), 0)
+    cols = lax.broadcasted_iota(jnp.int32, (B, B), 1)
+
+    @pl.loop(0, chan_count)
+    def _(chan):
+        base = chan * NBLK
+        for r in range(NBR):
+            both = packed[chan, r * NBR + r]
+            flip = both.T
+            zero = jnp.zeros_like(both)
+            eta_full[base + r * NBR + r] = jnp.where(rows < cols, both, jnp.where(rows > cols, -flip, zero))
+            ham_full[base + r * NBR + r] = jnp.where(rows >= cols, both, flip)
+            for s in range(r + 1, NBR):
+                high = packed[chan, r * NBR + s]
+                low = packed[chan, s * NBR + r]
+                eta_full[base + r * NBR + s] = high
+                eta_full[base + s * NBR + r] = -(high.T)
+                ham_full[base + s * NBR + r] = low
+                ham_full[base + r * NBR + s] = low.T
+
+    sums[...] = jnp.zeros_like(sums)
+    half = B // 2
+
+    @pl.loop(0, local_count)
+    def _(q):
+        @pl.loop(0, NBR)
+        def _(r):
+            for s in range(NBR):
+                for part in range(2):
+                    span = pl.ds(part * half, half)
+                    total_eta = jnp.zeros((half, B), jnp.float32)
+                    total_ham = jnp.zeros((half, B), jnp.float32)
+                    for term in range(K):
+                        at = (r * NBR + s) * K + term
+                        which = refs[q, at]
+                        weight = coef[q, at]
+                        total_eta += eta_full[which, span, :].astype(jnp.float32) * weight
+                        total_ham += ham_full[which, span, :].astype(jnp.float32) * weight
+                    band = pl.ds(pl.multiple_of(r * B + part * half, half), half)
+                    mix_eta[band, s * B : (s + 1) * B] = total_eta.astype(jnp.bfloat16)
+                    mix_ham[band, s * B : (s + 1) * B] = total_ham.astype(jnp.bfloat16)
+
+        scale = occ[q]
+
+        @pl.loop(0, NBR)
+        def _(r):
+            band = pl.ds(pl.multiple_of(r * B, B), B)
+            slab = jnp.dot(
+                mix_eta[band, :] * scale, mix_ham[...], preferred_element_type=jnp.float32
+            ) - jnp.dot(mix_ham[band, :] * scale, mix_eta[...], preferred_element_type=jnp.float32)
+            for s in range(NBR):
+                z_tiles[r * NBR + s] = slab[:, s * B : (s + 1) * B]
+
+        @pl.loop(0, 2 * K)
+        def _(slot):
+            at = picks[q, slot]
+            target = (slot // K) * NBLK + lax.rem(refs[q, at], NBLK)
+            back = (z_tiles[at // K] * coef[q, at]).astype(jnp.bfloat16)
+            sums[target] += back.astype(jnp.float32)
+
+    for r in range(NBR):
+        for s in range(NBR):
+            here = (slice(r * B, (r + 1) * B), slice(s * B, (s + 1) * B))
+            own_ref[here] = sums[r * NBR + s]
+            twin_ref[here] = sums[NBLK + r * NBR + s]
+
+
+def recouple(refs, coef, picks, packed, occ, order):
+    chan_count = packed.shape[0]
+    vmem = pl.BlockSpec(memory_space=pltpu.VMEM)
+    smem = pl.BlockSpec(memory_space=pltpu.SMEM)
+    return pl.pallas_call(
+        recouple_kernel,
+        out_shape=(jax.ShapeDtypeStruct((order, order), jnp.float32),) * 2,
+        in_specs=[smem, smem, smem, vmem, vmem],
+        out_specs=(vmem, vmem),
+        scratch_shapes=[
+            pltpu.VMEM((chan_count * NBLK, B, B), jnp.bfloat16),
+            pltpu.VMEM((chan_count * NBLK, B, B), jnp.bfloat16),
+            pltpu.VMEM((order, order), jnp.bfloat16),
+            pltpu.VMEM((order, order), jnp.bfloat16),
+            pltpu.VMEM((NBLK, B, B), jnp.float32),
+            pltpu.VMEM((2 * NBLK, B, B), jnp.float32),
+        ],
+        compiler_params=pltpu.CompilerParams(vmem_limit_bytes=LIMIT),
+    )(refs, coef, picks, packed, occ)
+
+
+def gather_plan(eta, ham, pp_occ, ph_occ, ph_src, coef6j):
+    chan_count = lax.axis_size("chan")
+    order = eta.shape[0]
+    me = lax.axis_index("chan")
+    core = me % 2
+    ladder_occ = (1 - pp_occ[0, 0] - pp_occ[0, 1]).astype(jnp.bfloat16)[None, :]
+    meta = jnp.concatenate(
+        [
+            ph_src.reshape(1, TERMS).astype(jnp.float32),
+            coef6j.reshape(1, TERMS),
+            (ph_occ[0, 0] - ph_occ[0, 1]).astype(jnp.float32).reshape(order // TERMS, TERMS),
+        ],
+        axis=0,
+    )
+    tables = lax.all_gather(meta, "chan", axis=0, tiled=False)
+    packed, ladder = gather_packed(eta, ham, ladder_occ, chan_count)
+    mine = lax.dynamic_index_in_dim(
+        tables.reshape(chan_count // 2, 2, -1, TERMS), core, axis=1, keepdims=False
+    )
+    refs = mine[:, 0].astype(jnp.int32)
+    coef = mine[:, 1]
+    occ = mine[:, 2:].reshape(-1, 1, order).astype(jnp.bfloat16)
+    twin = me + 1 - 2 * core
+    hits = refs[:, None, :] // NBLK == jnp.stack([me, twin])[None, :, None]
+    rank = jnp.cumsum(hits.astype(jnp.int32), axis=-1) - 1
+    slots = jnp.arange(K, dtype=jnp.int32)[None, None, :, None]
+    chosen = hits[:, :, None, :] & (rank[:, :, None, :] == slots)
+    picks = jnp.sum(
+        jnp.where(chosen, jnp.arange(TERMS, dtype=jnp.int32), 0), axis=-1
+    ).reshape(-1, 2 * K)
+    own, other = recouple(refs, coef, picks, packed, occ, order)
+    pairs = [(i, i + 1 - 2 * (i % 2)) for i in range(chan_count)]
+    received = lax.ppermute(other, "chan", pairs)
+    return ladder + own + received
+
+
 def solution(mesh):
+    chan_count = mesh.shape["chan"]
+    plan = gather_plan if chan_count == LEVELS * 4 else exchange_plan
     return jax.shard_map(
-        on_device,
+        plan,
         mesh=mesh,
         in_specs=(
             P(("groups", "chan"), None),

time: 380 us -> 123 us (0.32)
  the two profiles are of different devices: /device:TPU:11 before, /device:TPU:0 now
where the time goes in v1:
time: 123 us
  Pallas kernels  88.6 us (72%)
  blocking collectives  23.2 us (19%)
  other arithmetic  4.66 us (4%)
  local copies, waits for them, and re-layouts  3.24 us (3%)
  waiting for transfers between devices  2.29 us (2%)
    pallas_call x1, Pallas kernels, gather_packed(): pl.pallas_call(gather_kernel, out_shape=(jax.ShapeDtypeStruct((chan_count...  53.3 us
    pallas_call x1, Pallas kernels, recouple(): pl.pallas_call(recouple_kernel, out_shape=(jax.ShapeDtypeStruct((order, o...  35.4 us
    all_gather x1, blocking collectives, gather_plan(): tables = lax.all_gather(meta, 'chan', axis=0, tiled=False)  23.2 us
    unnamed x5, local copies, waits for them, and re-layouts  2.84 us
  transfers between devices with their start and end apart: 1, of which 1 were waited for; matrix products, arithmetic and copies ran while one was open for 0% of the time, Pallas kernels for 0%

profile of v1, /device:TPU:0, one launch (start us, length us, event | category | flops | bytes accessed | tf_op | source)
XLA Modules:
  0.0 122.6 jit_solution(3266593296971665957)
XLA Ops:
  0.0 0.8 subtract_convert_fusion
  0.8 0.7 convert_element_type.51
  1.5 0.1 copy.23
  1.5 0.1 convert_element_type.52
  1.6 0.8 copy.24
  2.4 0.1 reshape.98
  2.5 23.2 %all-gather.1 = f32[16,6,128]{2,1,0:T(8,128)S(1)} all-gather(f32[1,6,128]{2,1,0:T(8,128)S(1)} %maximum_bitcast_fusion), channel_id=2, replica_groups=mesh['groups'=2,'chan'=16] {'chan'}, dimensions={0}, use_global_device_ids=true | all-gather | bytes 52224 | tf_op jit(solution)/shard_map/all_gather | solution.py:372
  25.8 0.8 convert_bitcast_fusion.occ_ref
  26.6 0.1 pad_add_fusion
  26.7 0.1 fusion.6
  26.7 0.6 reduce_window_sum.11
  27.3 0.4 select_reduce_fusion
  27.7 0.1 reshape.100.picks
  27.8 0.0 copy-start
  27.8 1.0 copy-done
  28.9 0.0 copy-start.1
  28.9 1.0 copy-done.1
  29.9 53.3 %shard_map.64 = (bf16[16,16,128,128]{3,2,1,0:T(8,128)(2,1)}, f32[512,512]{1,0:T(8,128)S(1)}) custom-call(bf16[512,512]{1,0:T(8,128)(2,1)S(1)} %copy-done, bf16[512,512]{1,0:T(8,128)(2,1)S(1)} %copy-done.1, bf16[1,512]{1,0:T(2,128)(2,1)S(1)} %convert_bitcast_fusion.occ_ref), custom_call_target="tpu_custom_call" | custom-call | tf_op jit(solution)/shard_map/pallas_call | solution.py:245
  83.2 35.4 %shard_map.65 = (f32[512,512]{1,0:T(8,128)S(1)}, f32[512,512]{1,0:T(8,128)S(1)}) custom-call(s32[8,128]{1,0:T(8,128)S(1)} %get-tuple-element.16.refs, f32[8,128]{1,0:T(8,128)S(1)} %get-tuple-element.15.coef, s32[8,16]{1,0:T(8,128)S(1)} %reshape.100.picks, bf16[16,16,128,128]{3,2,1,0:T(8,128)(2,1)} %get-tuple-element.10.packed, bf16[8,1,512]{2,1,0:T(2,128)(2,1)S(1)} %copy.28.occ), custom_call_target="tpu_custom_call" | custom-call | tf_op jit(solution)/shard_map/pallas_call | solution.py:341
  118.5 0.4 collective-permute-start
  119.0 2.3 %collective-permute-done = f32[512,512]{1,0:T(8,128)S(1)} collective-permute-done((f32[512,512]{1,0:T(8,128)S(1)}, f32[512,512]{1,0:T(8,128)S(1)}, u32[]{:S(2)}, u32[]{:S(2)}) %collective-permute-start) | collective-permute-done | bytes 1048608 | tf_op jit(solution)/shard_map/ppermute | solution.py:390
  121.3 1.3 %add_add_fusion = f32[512,512]{1,0:T(8,128)} fusion(f32[512,512]{1,0:T(8,128)S(1)} %collective-permute-done, f32[512,512]{1,0:T(8,128)S(1)} %get-tuple-element.9, f32[512,512]{1,0:T(8,128)S(1)} %get-tuple-element.11), kind=kLoop, calls=%fused_computation | loop fusion | flops 524288 | bytes 4194304 | tf_op jit(solution)/shard_map/add | solution.py:391
  (10 shorter events, 0.1 us)
Async XLA Ops:
  27.8 1.0 copy-start
  28.9 1.0 copy-start.1
  118.5 2.7 %collective-permute-start = (f32[512,512]{1,0:T(8,128)S(1)}, f32[512,512]{1,0:T(8,128)S(1)}, u32[]{:S(2)}, u32[]{:S(2)}) collective-permute-start(f32[512,512]{1,0:T(8,128)S(1)} %get-tuple-element.12), channel_id=1, source_target_pairs={{0,1},{1,0},{2,3},{3,2},{4,5},{5,4},{6,7},{7,6},{8,9},{9,8},{10,11... | collective-permute-start | bytes 3145736 | tf_op jit(solution)/shard_map/ppermute | solution.py:390

commit v2 on v0

--- a/solution.py
+++ b/solution.py
@@ -1,15 +1,20 @@
 import jax
 import jax.numpy as jnp
 from jax import lax
+from jax.experimental import pallas as pl
+from jax.experimental.pallas import tpu as pltpu
 from jax.sharding import PartitionSpec as P
 
 B = 128
 NBR = 4
 K = 8
 NBLK = 16
-
-
-def on_device(eta, ham, pp_occ, ph_occ, ph_src, coef6j):
+TERMS = NBLK * K
+MESH = pl.DeviceIdType.MESH
+LIMIT = 48 * 1024 * 1024
+
+
+def exchange_plan(eta, ham, pp_occ, ph_occ, ph_src, coef6j):
     chan_count = lax.axis_size("chan")
     chan_order = eta.shape[0]
     tile_size = B
@@ -97,9 +102,378 @@
     return ladder + join_tiles(ph_term)
 
 
+LEVELS = 4
+HALVES = 2
+PER_HALF = NBLK // HALVES
+TABLE = 16
+CHUNK = PER_HALF * B + TABLE
+
+
+def flow_kernel(
+    eta_ref, ham_ref, pp_occ_ref, ph_occ_ref, src_ref, coef_ref, out_ref,
+    packed, eta_full, ham_full, left, right, z_tiles, outbound, inbound,
+    src_table, coef_table, pick_table, gain_table, refs, weights, picks, gains,
+    send_z, send_x, send_c, recv, local, send_sum, recv_sum,
+):
+    group = lax.axis_index("groups")
+    me = lax.axis_index("chan")
+    level = me // 4
+    side = (me // 2) % 2
+    core = me % 2
+    chan_count = packed.shape[0]
+    local_count = chan_count // 2
+
+    def chan_at(lvl, sd, cr):
+        return (lvl * 2 + sd) * 2 + cr
+
+    up = chan_at(level + 1, side, core)
+    down = chan_at(level - 1, side, core)
+    across = chan_at(level, 1 - side, core)
+    twin = chan_at(level, side, 1 - core)
+    has_up = level < LEVELS - 1
+    has_down = level > 0
+    mate = level + 1 - 2 * (level % 2)
+
+    barrier = pltpu.get_barrier_semaphore()
+
+    def greet(target):
+        pl.semaphore_signal(barrier, inc=1, device_id=(group, target), device_id_type=MESH)
+
+    greet(across)
+    greet(twin)
+
+    @pl.when(has_up)
+    def _():
+        greet(up)
+
+    @pl.when(has_down)
+    def _():
+        greet(down)
+
+    rows = lax.broadcasted_iota(jnp.int32, (B, B), 0)
+    cols = lax.broadcasted_iota(jnp.int32, (B, B), 1)
+
+    def tile_rows(block):
+        return block // PER_HALF, pl.ds((block % PER_HALF) * B, B)
+
+    for r in range(NBR):
+        for s in range(NBR):
+            here = (pl.ds(r * B, B), pl.ds(s * B, B))
+            if r < s:
+                tile = eta_ref[here]
+            elif r > s:
+                tile = ham_ref[here]
+            else:
+                tile = jnp.where(rows < cols, eta_ref[here], ham_ref[here])
+            half, band = tile_rows(r * NBR + s)
+            packed[me, half, band, :] = tile
+    coef = coef_ref[...]
+    first = coef.astype(jnp.bfloat16)
+    rest = coef - first.astype(jnp.float32)
+    second = rest.astype(jnp.bfloat16)
+    third = (rest - second.astype(jnp.float32)).astype(jnp.bfloat16)
+    table = jnp.concatenate(
+        [
+            src_ref[...].astype(jnp.float32),
+            first.astype(jnp.float32),
+            second.astype(jnp.float32),
+            third.astype(jnp.float32),
+            ph_occ_ref[...].astype(jnp.float32),
+            jnp.zeros((TABLE - 8, B), jnp.float32),
+        ],
+        axis=0,
+    )
+    for half in range(HALVES):
+        packed[me, half, PER_HALF * B :, :] = table.astype(jnp.bfloat16)
+
+    pl.semaphore_wait(barrier, 2 + has_up.astype(jnp.int32) + has_down.astype(jnp.int32))
+
+    def remote(src, half, sem, target):
+        return pltpu.make_async_remote_copy(
+            src_ref=packed.at[src, half],
+            dst_ref=packed.at[src, half],
+            send_sem=sem,
+            recv_sem=recv.at[src, half],
+            device_id=(group, target),
+            device_id_type=MESH,
+        )
+
+    def arrived(src, half):
+        remote(src, half, send_c.at[0, 0, 0, 0], twin).wait_recv()
+
+    def moves(step, way, lvl, half, act):
+        src = chan_at(lvl, side, core)
+        if step == 0 or way == 0:
+            @pl.when(has_up)
+            def _():
+                act(remote(src, half, send_z.at[0, step, half], up))
+        if step == 0 or way == 1:
+            @pl.when(has_down)
+            def _():
+                act(remote(src, half, send_z.at[1, step, half], down))
+        if half == 1 and step == 1:
+            @pl.when(lvl != mate)
+            def _():
+                act(remote(src, half, send_x.at[way, step, half], across))
+        else:
+            act(remote(src, half, send_x.at[way, step, half], across))
+        act(remote(src, half, send_c.at[0, way, step, half], twin))
+
+    def across_moves(step, way, lvl, half, act):
+        src = chan_at(lvl, 1 - side, core)
+        act(remote(src, half, send_c.at[1, way, step, half], twin))
+        if half == 1 and step == 0:
+            act(remote(src, half, send_z.at[0, LEVELS, half], chan_at(mate, side, core)))
+
+    def each_way(step, action):
+        for way in range(2 if step else 1):
+            lvl = level - step if way == 0 else level + step
+            inside = lvl >= 0 if way == 0 else lvl < LEVELS
+
+            @pl.when(inside)
+            def _():
+                action(way, lvl)
+
+    def column(step):
+        for half in range(HALVES):
+            def action(way, lvl):
+                if step:
+                    arrived(chan_at(lvl, side, core), half)
+                moves(step, way, lvl, half, lambda copy: copy.start())
+
+            each_way(step, action)
+
+    def crossing(step):
+        for half in range(HALVES):
+            def action(way, lvl):
+                arrived(chan_at(lvl, 1 - side, core), half)
+                across_moves(step, way, lvl, half, lambda copy: copy.start())
+
+            each_way(step, action)
+
+    def expand(src):
+        base = src * NBLK
+        for r in range(NBR):
+            for s in range(NBR):
+                half, band = tile_rows(r * NBR + s)
+                tile = packed[src, half, band, :]
+                flip = tile.T
+                if r < s:
+                    eta_full[base + r * NBR + s] = tile
+                    eta_full[base + s * NBR + r] = -flip
+                elif r > s:
+                    ham_full[base + r * NBR + s] = tile
+                    ham_full[base + s * NBR + r] = flip
+                else:
+                    zero = jnp.zeros_like(tile)
+                    eta_full[base + r * NBR + s] = jnp.where(
+                        rows < cols, tile, jnp.where(rows > cols, -flip, zero)
+                    )
+                    ham_full[base + r * NBR + s] = jnp.where(rows >= cols, tile, flip)
+
+    def expand_all(step, members):
+        ways = 2 if step else 1
+
+        @pl.loop(0, ways * len(members))
+        def _(turn):
+            way = turn % ways
+            lvl = level + (2 * way - 1) * step
+
+            @pl.when((lvl >= 0) & (lvl < LEVELS))
+            def _():
+                place = members[0] if len(members) == 1 else turn // ways
+                if len(members) == 1:
+                    sd, cr = place
+                    src = chan_at(lvl, sd, cr)
+                else:
+                    src = chan_at(lvl, place, 1 - core)
+                    for half in range(HALVES):
+                        arrived(src, half)
+                expand(src)
+
+    def expand_twin(step):
+        expand_all(step, (0, 1))
+
+    column(0)
+    occ = pp_occ_ref[...]
+    for r in range(NBR):
+        band = pl.ds(r * B, B)
+        out_ref[band, :] = jnp.dot(
+            eta_ref[band, :] * occ, ham_ref[...], preferred_element_type=jnp.float32
+        ) - jnp.dot(ham_ref[band, :] * occ, eta_ref[...], preferred_element_type=jnp.float32)
+    expand_all(0, ((side, core),))
+    for step in range(1, LEVELS):
+        column(step)
+        crossing(step - 1)
+        expand_all(step, ((side, core),))
+        expand_all(step - 1, ((1 - side, core),))
+        if step >= 2:
+            expand_twin(step - 2)
+    crossing(LEVELS - 1)
+    expand_twin(LEVELS - 2)
+    expand_all(LEVELS - 1, ((1 - side, core),))
+    expand_twin(LEVELS - 1)
+
+    for q in range(local_count):
+        table = packed[2 * q + core, 0, PER_HALF * B :, :].astype(jnp.float32)
+        src_table[q : q + 1, :] = jnp.clip(
+            table[0:1, :].astype(jnp.int32), 0, chan_count * NBLK - 1
+        )
+        coef_table[q : q + 1, :] = table[1:2, :] + (table[2:3, :] + table[3:4, :])
+    loads = [
+        pltpu.make_async_copy(src_table, refs, local.at[0]),
+        pltpu.make_async_copy(coef_table, weights, local.at[1]),
+    ]
+    for load in loads:
+        load.start()
+    named = src_table[...]
+    factor = coef_table[...]
+    lanes = lax.broadcasted_iota(jnp.int32, named.shape, 1)
+    found = jnp.zeros(named.shape, jnp.int32)
+    gain = jnp.zeros(named.shape, jnp.float32)
+    for place in range(2 * NBLK):
+        owner = me if place < NBLK else twin
+        hit = named == owner * NBLK + place % NBLK
+        tile = jnp.max(jnp.where(hit, lanes // K, 0), axis=1, keepdims=True)
+        scale = jnp.sum(jnp.where(hit, factor, 0.0), axis=1, keepdims=True)
+        found = jnp.where(lanes == place, tile, found)
+        gain = jnp.where(lanes == place, scale, gain)
+    pick_table[...] = found
+    gain_table[...] = gain
+    more = [
+        pltpu.make_async_copy(pick_table, picks, local.at[2]),
+        pltpu.make_async_copy(gain_table, gains, local.at[3]),
+    ]
+    for load in more:
+        load.start()
+    for load in loads:
+        load.wait()
+
+    part_rows = B // 2
+    order = NBR * B
+
+    @pl.loop(0, local_count)
+    def _(q):
+        @pl.loop(0, NBR)
+        def _(r):
+            for s in range(NBR):
+                scale = packed[2 * q + core, 0, PER_HALF * B :, :][4 + s : 5 + s, :]
+                for part in range(2):
+                    span = pl.ds(part * part_rows, part_rows)
+                    total_eta = jnp.zeros((part_rows, B), jnp.float32)
+                    total_ham = jnp.zeros((part_rows, B), jnp.float32)
+                    for term in range(K):
+                        at = (r * NBR + s) * K + term
+                        which = refs[q, at]
+                        weight = weights[q, at]
+                        total_eta += eta_full[which, span, :].astype(jnp.float32) * weight
+                        total_ham += ham_full[which, span, :].astype(jnp.float32) * weight
+                    start = pl.multiple_of(r * B + part * part_rows, part_rows)
+                    lane = slice(s * B, (s + 1) * B)
+                    beyond = slice(order + s * B, order + (s + 1) * B)
+                    mixed_eta = total_eta.astype(jnp.bfloat16)
+                    mixed_ham = total_ham.astype(jnp.bfloat16)
+                    left[pl.ds(start, part_rows), lane] = mixed_eta * scale
+                    left[pl.ds(start, part_rows), beyond] = -(mixed_ham * scale)
+                    right[pl.ds(start, part_rows), lane] = mixed_ham
+                    right[pl.ds(order + start, part_rows), lane] = mixed_eta
+
+        @pl.loop(0, NBR)
+        def _(r):
+            band = pl.ds(pl.multiple_of(r * B, B), B)
+            slab = jnp.dot(left[band, :], right[...], preferred_element_type=jnp.float32)
+            for s in range(NBR):
+                z_tiles[q * NBLK + r * NBR + s] = slab[:, s * B : (s + 1) * B]
+
+    for load in more:
+        load.wait()
+
+    def sum_back(first, target, keep):
+        @pl.loop(0, NBR)
+        def _(r):
+            for s in range(NBR):
+                for part in range(2):
+                    span = pl.ds(part * part_rows, part_rows)
+                    total = jnp.zeros((part_rows, B), jnp.float32)
+                    for q in range(local_count):
+                        at = first + r * NBR + s
+                        tile = z_tiles[q * NBLK + picks[q, at], span, :]
+                        total += (tile * gains[q, at]).astype(jnp.bfloat16).astype(jnp.float32)
+                    start = pl.multiple_of(r * B + part * part_rows, part_rows)
+                    here = (pl.ds(start, part_rows), slice(s * B, (s + 1) * B))
+                    target[here] = target[here] + total if keep else total
+
+    sum_back(NBLK, outbound, False)
+    swap = pltpu.make_async_remote_copy(
+        src_ref=outbound,
+        dst_ref=inbound,
+        send_sem=send_sum,
+        recv_sem=recv_sum,
+        device_id=(group, twin),
+        device_id_type=MESH,
+    )
+    swap.start()
+    sum_back(0, out_ref, True)
+
+    for step in range(LEVELS):
+        for half in range(HALVES):
+            each_way(step, lambda way, lvl: moves(step, way, lvl, half, lambda copy: copy.wait_send()))
+            each_way(
+                step, lambda way, lvl: across_moves(step, way, lvl, half, lambda copy: copy.wait_send())
+            )
+    swap.wait()
+    out_ref[...] += inbound[...]
+
+
+def gather_plan(eta, ham, pp_occ, ph_occ, ph_src, coef6j):
+    chan_count = lax.axis_size("chan")
+    order = eta.shape[0]
+    pp_scale = (1 - pp_occ[0, 0] - pp_occ[0, 1]).astype(jnp.bfloat16)[None, :]
+    ph_scale = (ph_occ[0, 0] - ph_occ[0, 1]).reshape(NBR, B)
+    vmem = pl.BlockSpec(memory_space=pltpu.VMEM)
+    blocks = chan_count * NBLK
+    mine = chan_count // 2
+    return pl.pallas_call(
+        flow_kernel,
+        out_shape=jax.ShapeDtypeStruct((order, order), jnp.float32),
+        in_specs=[vmem] * 6,
+        out_specs=vmem,
+        scratch_shapes=[
+            pltpu.VMEM((chan_count, HALVES, CHUNK, B), jnp.bfloat16),
+            pltpu.VMEM((blocks, B, B), jnp.bfloat16),
+            pltpu.VMEM((blocks, B, B), jnp.bfloat16),
+            pltpu.VMEM((order, 2 * order), jnp.bfloat16),
+            pltpu.VMEM((2 * order, order), jnp.bfloat16),
+            pltpu.VMEM((mine * NBLK, B, B), jnp.float32),
+            pltpu.VMEM((order, order), jnp.float32),
+            pltpu.VMEM((order, order), jnp.float32),
+            pltpu.VMEM((mine, TERMS), jnp.int32),
+            pltpu.VMEM((mine, TERMS), jnp.float32),
+            pltpu.VMEM((mine, TERMS), jnp.int32),
+            pltpu.VMEM((mine, TERMS), jnp.float32),
+            pltpu.SMEM((mine, TERMS), jnp.int32),
+            pltpu.SMEM((mine, TERMS), jnp.float32),
+            pltpu.SMEM((mine, TERMS), jnp.int32),
+            pltpu.SMEM((mine, TERMS), jnp.float32),
+            pltpu.SemaphoreType.DMA((2, LEVELS + 1, HALVES)),
+            pltpu.SemaphoreType.DMA((2, LEVELS, HALVES)),
+            pltpu.SemaphoreType.DMA((2, 2, LEVELS, HALVES)),
+            pltpu.SemaphoreType.DMA((chan_count, HALVES)),
+            pltpu.SemaphoreType.DMA((4,)),
+            pltpu.SemaphoreType.DMA,
+            pltpu.SemaphoreType.DMA,
+        ],
+        compiler_params=pltpu.CompilerParams(
+            collective_id=0, has_side_effects=True, vmem_limit_bytes=LIMIT
+        ),
+    )(eta, ham, pp_scale, ph_scale, ph_src.reshape(1, TERMS), coef6j.reshape(1, TERMS))
+
+
 def solution(mesh):
+    chan_count = mesh.shape["chan"]
+    plan = gather_plan if chan_count == LEVELS * 4 else exchange_plan
     return jax.shard_map(
-        on_device,
+        plan,
         mesh=mesh,
         in_specs=(
             P(("groups", "chan"), None),

time: 380 us -> 90.6 us (0.24)
  the two profiles are of different devices: /device:TPU:11 before, /device:TPU:0 now
where the time goes in v2:
time: 90.6 us; the launch traced here: 90.3 us
  Pallas kernels  84.8 us (94%)
  local copies, waits for them, and re-layouts  4.64 us (5%)
    pallas_call x1, Pallas kernels, gather_plan(): pl.pallas_call(flow_kernel, out_shape=jax.ShapeDtypeStruct((order, order)...  84.8 us
    unnamed x13, local copies, waits for them, and re-layouts  4.47 us

profile of v2, /device:TPU:0, one launch (start us, length us, event | category | flops | bytes accessed | tf_op | source)
XLA Modules:
  0.0 90.3 jit_solution(1567504899613435726)
XLA Ops:
  0.0 0.0 copy-start.4
  0.0 0.8 convert_bitcast_fusion.pp_occ_ref
  0.8 0.0 copy-done.4
  0.8 0.0 copy-start.2
  0.8 0.7 copy-done.2
  1.5 0.1 copy.9
  1.5 0.0 copy-start.3
  1.5 0.1 reshape.37.src_ref
  1.6 0.6 copy-done.3
  2.2 0.1 copy.10
  2.3 0.1 reshape.38.coef_ref
  2.4 0.0 copy-start
  2.4 1.0 %copy-done = bf16[512,512]{1,0:T(8,128)(2,1)S(1)} copy-done((bf16[512,512]{1,0:T(8,128)(2,1)S(1)}, bf16[512,512]{1,0:T(8,128)(2,1)}, u32[]{:S(2)}) %copy-start) | copy-done | bytes 524312
  3.4 0.0 copy-start.1
  3.4 1.0 %copy-done.1 = bf16[512,512]{1,0:T(8,128)(2,1)S(1)} copy-done((bf16[512,512]{1,0:T(8,128)(2,1)S(1)}, bf16[512,512]{1,0:T(8,128)(2,1)}, u32[]{:S(2)}) %copy-start.1) | copy-done | bytes 524312
  4.5 84.8 %shard_map.64 = f32[512,512]{1,0:T(8,128)S(1)} custom-call(bf16[512,512]{1,0:T(8,128)(2,1)S(1)} %copy-done, bf16[512,512]{1,0:T(8,128)(2,1)S(1)} %copy-done.1, bf16[1,512]{1,0:T(2,128)(2,1)S(1)} %convert_bitcast_fusion.pp_occ_ref, s32[4,128]{1,0:T(4,128)S(1)} %bitcast.3, s32[1,128]{1,0:T(1,128)S(1)} %reshape.37.src_ref, f32[1,128]{1,0:T(1,128)S(1)} %reshape.38.coef_ref), custom_call_target="tpu_custom_call" | custom-call | tf_op jit(solution)/shard_map/pallas_call | solution.py:436
  89.3 1.0 %copy.12 = f32[512,512]{1,0:T(8,128)} copy(f32[512,512]{1,0:T(8,128)S(1)} %shard_map.64) | data formatting | bytes 2097152
  (1 shorter events, 0.0 us)
Async XLA Ops:
  0.0 0.8 copy-start.4
  0.8 0.7 copy-start.2
  1.5 0.7 copy-start.3
  2.4 1.0 %copy-start = (bf16[512,512]{1,0:T(8,128)(2,1)S(1)}, bf16[512,512]{1,0:T(8,128)(2,1)}, u32[]{:S(2)}) copy-start(bf16[512,512]{1,0:T(8,128)(2,1)} %eta_ref.1) | copy-start | bytes 1572868
  3.4 1.0 %copy-start.1 = (bf16[512,512]{1,0:T(8,128)(2,1)S(1)}, bf16[512,512]{1,0:T(8,128)(2,1)}, u32[]{:S(2)}) copy-start(bf16[512,512]{1,0:T(8,128)(2,1)} %ham_ref.1) | copy-start | bytes 1572868

commit v3 on v2

--- a/solution.py
+++ b/solution.py
@@ -11,7 +11,7 @@
 NBLK = 16
 TERMS = NBLK * K
 MESH = pl.DeviceIdType.MESH
-LIMIT = 48 * 1024 * 1024
+LIMIT = 60 * 1024 * 1024
 
 
 def exchange_plan(eta, ham, pp_occ, ph_occ, ph_src, coef6j):
@@ -109,11 +109,15 @@
 CHUNK = PER_HALF * B + TABLE
 
 
+def flat(values):
+    return jnp.concatenate([values[k : k + 1, :] for k in range(K)], axis=1)
+
+
 def flow_kernel(
-    eta_ref, ham_ref, pp_occ_ref, ph_occ_ref, src_ref, coef_ref, out_ref,
-    packed, eta_full, ham_full, left, right, z_tiles, outbound, inbound,
+    eta_hbm, ham_hbm, pp_occ_hbm, ph_occ_hbm, src_hbm, coef_hbm, out_ref,
+    eta_ref, ham_ref, pp_occ_ref, ph_occ_ref, src_ref, coef_ref, packed, eta_full, ham_full, left, right, z_tiles, outbound, inbound,
     src_table, coef_table, pick_table, gain_table, refs, weights, picks, gains,
-    send_z, send_x, send_c, recv, local, send_sum, recv_sum,
+    send_z, send_x, send_c, recv, local, fetch, send_sum, recv_sum,
 ):
     group = lax.axis_index("groups")
     me = lax.axis_index("chan")
@@ -150,12 +154,22 @@
     def _():
         greet(down)
 
+    inputs = (eta_hbm, ham_hbm, src_hbm, coef_hbm, ph_occ_hbm, pp_occ_hbm)
+    places = (eta_ref, ham_ref, src_ref, coef_ref, ph_occ_ref, pp_occ_ref)
+    fetches = [
+        pltpu.make_async_copy(there, here, fetch.at[i])
+        for i, (there, here) in enumerate(zip(inputs, places))
+    ]
+    for copy in fetches:
+        copy.start()
     rows = lax.broadcasted_iota(jnp.int32, (B, B), 0)
     cols = lax.broadcasted_iota(jnp.int32, (B, B), 1)
 
     def tile_rows(block):
         return block // PER_HALF, pl.ds((block % PER_HALF) * B, B)
 
+    for copy in fetches:
+        copy.wait()
     for r in range(NBR):
         for s in range(NBR):
             here = (pl.ds(r * B, B), pl.ds(s * B, B))
@@ -167,18 +181,19 @@
                 tile = jnp.where(rows < cols, eta_ref[here], ham_ref[here])
             half, band = tile_rows(r * NBR + s)
             packed[me, half, band, :] = tile
-    coef = coef_ref[...]
+    coef = flat(coef_ref[...])
     first = coef.astype(jnp.bfloat16)
     rest = coef - first.astype(jnp.float32)
     second = rest.astype(jnp.bfloat16)
     third = (rest - second.astype(jnp.float32)).astype(jnp.bfloat16)
+    occ_row = (ph_occ_ref[0:1, :] - ph_occ_ref[1:2, :]).astype(jnp.float32)
     table = jnp.concatenate(
         [
-            src_ref[...].astype(jnp.float32),
+            flat(src_ref[...].astype(jnp.float32)),
             first.astype(jnp.float32),
             second.astype(jnp.float32),
             third.astype(jnp.float32),
-            ph_occ_ref[...].astype(jnp.float32),
+            *[occ_row[:, s * B : (s + 1) * B] for s in range(NBR)],
             jnp.zeros((TABLE - 8, B), jnp.float32),
         ],
         axis=0,
@@ -211,7 +226,7 @@
             @pl.when(has_down)
             def _():
                 act(remote(src, half, send_z.at[1, step, half], down))
-        if half == 1 and step == 1:
+        if half >= HALVES // 2 and step == 1:
             @pl.when(lvl != mate)
             def _():
                 act(remote(src, half, send_x.at[way, step, half], across))
@@ -222,7 +237,7 @@
     def across_moves(step, way, lvl, half, act):
         src = chan_at(lvl, 1 - side, core)
         act(remote(src, half, send_c.at[1, way, step, half], twin))
-        if half == 1 and step == 0:
+        if half >= HALVES // 2 and step == 0:
             act(remote(src, half, send_z.at[0, LEVELS, half], chan_at(mate, side, core)))
 
     def each_way(step, action):
@@ -243,8 +258,8 @@
 
             each_way(step, action)
 
-    def crossing(step):
-        for half in range(HALVES):
+    def crossing(step, begin=0, end=HALVES):
+        for half in range(begin, end):
             def action(way, lvl):
                 arrived(chan_at(lvl, 1 - side, core), half)
                 across_moves(step, way, lvl, half, lambda copy: copy.start())
@@ -256,7 +271,7 @@
         for r in range(NBR):
             for s in range(NBR):
                 half, band = tile_rows(r * NBR + s)
-                tile = packed[src, half, band, :]
+                tile = packed[src, half, band, :].astype(jnp.float32)
                 flip = tile.T
                 if r < s:
                     eta_full[base + r * NBR + s] = tile
@@ -295,7 +310,7 @@
         expand_all(step, (0, 1))
 
     column(0)
-    occ = pp_occ_ref[...]
+    occ = (1 - pp_occ_ref[0:1, :] - pp_occ_ref[1:2, :]).astype(jnp.bfloat16)
     for r in range(NBR):
         band = pl.ds(r * B, B)
         out_ref[band, :] = jnp.dot(
@@ -309,11 +324,7 @@
         expand_all(step - 1, ((1 - side, core),))
         if step >= 2:
             expand_twin(step - 2)
-    crossing(LEVELS - 1)
-    expand_twin(LEVELS - 2)
-    expand_all(LEVELS - 1, ((1 - side, core),))
-    expand_twin(LEVELS - 1)
-
+    crossing(LEVELS - 1, 0, 1)
     for q in range(local_count):
         table = packed[2 * q + core, 0, PER_HALF * B :, :].astype(jnp.float32)
         src_table[q : q + 1, :] = jnp.clip(
@@ -334,7 +345,7 @@
     for place in range(2 * NBLK):
         owner = me if place < NBLK else twin
         hit = named == owner * NBLK + place % NBLK
-        tile = jnp.max(jnp.where(hit, lanes // K, 0), axis=1, keepdims=True)
+        tile = jnp.max(jnp.where(hit, lanes % NBLK, 0), axis=1, keepdims=True)
         scale = jnp.sum(jnp.where(hit, factor, 0.0), axis=1, keepdims=True)
         found = jnp.where(lanes == place, tile, found)
         gain = jnp.where(lanes == place, scale, gain)
@@ -346,6 +357,11 @@
     ]
     for load in more:
         load.start()
+    crossing(LEVELS - 1, 1, HALVES)
+    expand_twin(LEVELS - 2)
+    expand_all(LEVELS - 1, ((1 - side, core),))
+    expand_twin(LEVELS - 1)
+
     for load in loads:
         load.wait()
 
@@ -363,11 +379,11 @@
                     total_eta = jnp.zeros((part_rows, B), jnp.float32)
                     total_ham = jnp.zeros((part_rows, B), jnp.float32)
                     for term in range(K):
-                        at = (r * NBR + s) * K + term
+                        at = term * NBLK + r * NBR + s
                         which = refs[q, at]
                         weight = weights[q, at]
-                        total_eta += eta_full[which, span, :].astype(jnp.float32) * weight
-                        total_ham += ham_full[which, span, :].astype(jnp.float32) * weight
+                        total_eta += eta_full[which, span, :] * weight
+                        total_ham += ham_full[which, span, :] * weight
                     start = pl.multiple_of(r * B + part * part_rows, part_rows)
                     lane = slice(s * B, (s + 1) * B)
                     beyond = slice(order + s * B, order + (s + 1) * B)
@@ -378,42 +394,48 @@
                     right[pl.ds(start, part_rows), lane] = mixed_ham
                     right[pl.ds(order + start, part_rows), lane] = mixed_eta
 
-        @pl.loop(0, NBR)
-        def _(r):
-            band = pl.ds(pl.multiple_of(r * B, B), B)
-            slab = jnp.dot(left[band, :], right[...], preferred_element_type=jnp.float32)
-            for s in range(NBR):
-                z_tiles[q * NBLK + r * NBR + s] = slab[:, s * B : (s + 1) * B]
+        for pair in range(NBR // 2):
+            lane = slice(2 * pair * B, 2 * (pair + 1) * B)
+            slab = jnp.dot(left[...], right[:, lane], preferred_element_type=jnp.float32)
+            for r in range(NBR):
+                for s in range(2):
+                    z_tiles[q * NBLK + r * NBR + 2 * pair + s] = slab[
+                        r * B : (r + 1) * B, s * B : (s + 1) * B
+                    ]
 
     for load in more:
         load.wait()
 
-    def sum_back(first, target, keep):
-        @pl.loop(0, NBR)
-        def _(r):
-            for s in range(NBR):
-                for part in range(2):
-                    span = pl.ds(part * part_rows, part_rows)
-                    total = jnp.zeros((part_rows, B), jnp.float32)
-                    for q in range(local_count):
-                        at = first + r * NBR + s
-                        tile = z_tiles[q * NBLK + picks[q, at], span, :]
-                        total += (tile * gains[q, at]).astype(jnp.bfloat16).astype(jnp.float32)
-                    start = pl.multiple_of(r * B + part * part_rows, part_rows)
-                    here = (pl.ds(start, part_rows), slice(s * B, (s + 1) * B))
-                    target[here] = target[here] + total if keep else total
-
-    sum_back(NBLK, outbound, False)
-    swap = pltpu.make_async_remote_copy(
-        src_ref=outbound,
-        dst_ref=inbound,
-        send_sem=send_sum,
-        recv_sem=recv_sum,
-        device_id=(group, twin),
-        device_id_type=MESH,
-    )
-    swap.start()
-    sum_back(0, out_ref, True)
+    def sum_back(first, target, r, keep):
+        for s in range(NBR):
+            for part in range(2):
+                span = pl.ds(part * part_rows, part_rows)
+                total = jnp.zeros((part_rows, B), jnp.float32)
+                for q in range(local_count):
+                    at = first + r * NBR + s
+                    tile = z_tiles[q * NBLK + picks[q, at], span, :]
+                    total += tile * gains[q, at]
+                here = (
+                    slice(r * B + part * part_rows, r * B + (part + 1) * part_rows),
+                    slice(s * B, (s + 1) * B),
+                )
+                target[here] = target[here] + total if keep else total
+
+    swaps = []
+    for r in range(NBR):
+        sum_back(NBLK, outbound, r, False)
+        swap = pltpu.make_async_remote_copy(
+            src_ref=outbound.at[pl.ds(r * B, B)],
+            dst_ref=inbound.at[pl.ds(r * B, B)],
+            send_sem=send_sum.at[r],
+            recv_sem=recv_sum.at[r],
+            device_id=(group, twin),
+            device_id_type=MESH,
+        )
+        swap.start()
+        swaps.append(swap)
+    for r in range(NBR):
+        sum_back(0, out_ref, r, True)
 
     for step in range(LEVELS):
         for half in range(HALVES):
@@ -421,27 +443,33 @@
             each_way(
                 step, lambda way, lvl: across_moves(step, way, lvl, half, lambda copy: copy.wait_send())
             )
-    swap.wait()
-    out_ref[...] += inbound[...]
+    for r, swap in enumerate(swaps):
+        swap.wait()
+        band = slice(r * B, (r + 1) * B)
+        out_ref[band, :] += inbound[band, :]
 
 
 def gather_plan(eta, ham, pp_occ, ph_occ, ph_src, coef6j):
     chan_count = lax.axis_size("chan")
     order = eta.shape[0]
-    pp_scale = (1 - pp_occ[0, 0] - pp_occ[0, 1]).astype(jnp.bfloat16)[None, :]
-    ph_scale = (ph_occ[0, 0] - ph_occ[0, 1]).reshape(NBR, B)
     vmem = pl.BlockSpec(memory_space=pltpu.VMEM)
     blocks = chan_count * NBLK
     mine = chan_count // 2
     return pl.pallas_call(
         flow_kernel,
         out_shape=jax.ShapeDtypeStruct((order, order), jnp.float32),
-        in_specs=[vmem] * 6,
+        in_specs=[pl.BlockSpec(memory_space=pl.ANY)] * 6,
         out_specs=vmem,
         scratch_shapes=[
+            pltpu.VMEM((order, order), jnp.bfloat16),
+            pltpu.VMEM((order, order), jnp.bfloat16),
+            pltpu.VMEM((2, order), jnp.int32),
+            pltpu.VMEM((2, order), jnp.int32),
+            pltpu.VMEM((K, NBLK), jnp.int32),
+            pltpu.VMEM((K, NBLK), jnp.float32),
             pltpu.VMEM((chan_count, HALVES, CHUNK, B), jnp.bfloat16),
-            pltpu.VMEM((blocks, B, B), jnp.bfloat16),
-            pltpu.VMEM((blocks, B, B), jnp.bfloat16),
+            pltpu.VMEM((blocks, B, B), jnp.float32),
+            pltpu.VMEM((blocks, B, B), jnp.float32),
             pltpu.VMEM((order, 2 * order), jnp.bfloat16),
             pltpu.VMEM((2 * order, order), jnp.bfloat16),
             pltpu.VMEM((mine * NBLK, B, B), jnp.float32),
@@ -460,13 +488,21 @@
             pltpu.SemaphoreType.DMA((2, 2, LEVELS, HALVES)),
             pltpu.SemaphoreType.DMA((chan_count, HALVES)),
             pltpu.SemaphoreType.DMA((4,)),
-            pltpu.SemaphoreType.DMA,
-            pltpu.SemaphoreType.DMA,
+            pltpu.SemaphoreType.DMA((6,)),
+            pltpu.SemaphoreType.DMA((NBR,)),
+            pltpu.SemaphoreType.DMA((NBR,)),
         ],
         compiler_params=pltpu.CompilerParams(
             collective_id=0, has_side_effects=True, vmem_limit_bytes=LIMIT
         ),
-    )(eta, ham, pp_scale, ph_scale, ph_src.reshape(1, TERMS), coef6j.reshape(1, TERMS))
+    )(
+        eta,
+        ham,
+        pp_occ[0],
+        ph_occ[0],
+        jnp.swapaxes(ph_src, 1, 2)[0],
+        jnp.swapaxes(coef6j, 1, 2)[0],
+    )
 
 
 def solution(mesh):

time: 90.6 us -> 78.3 us (0.86)
  Pallas kernels: 84.8 us -> 75.8 us
  local copies, waits for them, and re-layouts: 4.64 us -> 2.26 us
    pallas_call x1, Pallas kernels: 84.8 us -> 75.8 us  [gather_plan(): pl.pallas_call(flow_kernel, out_shape=jax.ShapeDtypeStruct((order, order)...]
    unnamed x13 -> x1, local copies, waits for them, and re-layouts: 4.47 us -> 2.26 us
where the time goes in v3:
time: 78.3 us; the launch traced here: 78.1 us
  Pallas kernels  75.8 us (97%)
  local copies, waits for them, and re-layouts  2.26 us (3%)
    pallas_call x1, Pallas kernels, gather_plan(): pl.pallas_call(flow_kernel, out_shape=jax.ShapeDtypeStruct((order, order)...  75.8 us
    unnamed x1, local copies, waits for them, and re-layouts  2.26 us

profile of v3, /device:TPU:0, one launch (start us, length us, event | category | flops | bytes accessed | tf_op | source)
XLA Modules:
  0.0 78.1 jit_solution(14921149248424098419)
XLA Ops:
  0.0 75.8 %shard_map.64 = f32[512,512]{1,0:T(8,128)} custom-call(bf16[512,512]{1,0:T(8,128)(2,1)} %eta_hbm.1, bf16[512,512]{1,0:T(8,128)(2,1)} %ham_hbm.1, s32[2,512]{1,0:T(2,128)} %bitcast.8, s32[2,512]{1,0:T(2,128)} %bitcast.9, s32[8,16]{1,0:T(8,128)} %bitcast.10, f32[8,16]{1,0:T(8,128)} %bitcast.11), custom_call_target="tpu_custom_call" | custom-call | tf_op jit(solution)/shard_map/pallas_call | solution.py:458
  75.9 2.3 %copy.8 = f32[512,512]{1,0:T(8,128)} copy(f32[512,512]{1,0:T(8,128)} %shard_map.64) | data formatting | bytes 2097152

commit v4 on v3

--- a/solution.py
+++ b/solution.py
@@ -237,8 +237,10 @@
     def across_moves(step, way, lvl, half, act):
         src = chan_at(lvl, 1 - side, core)
         act(remote(src, half, send_c.at[1, way, step, half], twin))
-        if half >= HALVES // 2 and step == 0:
-            act(remote(src, half, send_z.at[0, LEVELS, half], chan_at(mate, side, core)))
+
+    def mate_moves(act):
+        for half in range(HALVES // 2, HALVES):
+            act(remote(across, half, send_z.at[0, LEVELS, half], chan_at(mate, side, core)))
 
     def each_way(step, action):
         for way in range(2 if step else 1):
@@ -261,10 +263,24 @@
     def crossing(step, begin=0, end=HALVES):
         for half in range(begin, end):
             def action(way, lvl):
-                arrived(chan_at(lvl, 1 - side, core), half)
-                across_moves(step, way, lvl, half, lambda copy: copy.start())
+                @pl.when((step != 1) | (half < HALVES // 2) | (lvl != mate))
+                def _():
+                    arrived(chan_at(lvl, 1 - side, core), half)
+                    across_moves(step, way, lvl, half, lambda copy: copy.start())
 
             each_way(step, action)
+
+    def crossing_mate():
+        way = (mate - level + 1) // 2
+        for half in range(HALVES // 2, HALVES):
+            arrived(chan_at(mate, 1 - side, core), half)
+            across_moves(1, way, mate, half, lambda copy: copy.start())
+
+    def expand_mate():
+        expand(chan_at(mate, 1 - side, core))
+        for half in range(HALVES):
+            arrived(chan_at(mate, 1 - side, 1 - core), half)
+        expand(chan_at(mate, 1 - side, 1 - core))
 
     def expand(src):
         base = src * NBLK
@@ -294,7 +310,10 @@
             way = turn % ways
             lvl = level + (2 * way - 1) * step
 
-            @pl.when((lvl >= 0) & (lvl < LEVELS))
+            facing = members[0][0] if len(members) == 1 else turn // ways
+            later = (facing != side) & (lvl == mate)
+
+            @pl.when((lvl >= 0) & (lvl < LEVELS) & jnp.logical_not(later))
             def _():
                 place = members[0] if len(members) == 1 else turn // ways
                 if len(members) == 1:
@@ -319,6 +338,8 @@
     expand_all(0, ((side, core),))
     for step in range(1, LEVELS):
         column(step)
+        if step == LEVELS - 1:
+            mate_moves(lambda copy: copy.start())
         crossing(step - 1)
         expand_all(step, ((side, core),))
         expand_all(step - 1, ((1 - side, core),))
@@ -358,9 +379,11 @@
     for load in more:
         load.start()
     crossing(LEVELS - 1, 1, HALVES)
+    crossing_mate()
     expand_twin(LEVELS - 2)
     expand_all(LEVELS - 1, ((1 - side, core),))
     expand_twin(LEVELS - 1)
+    expand_mate()
 
     for load in loads:
         load.wait()
@@ -443,6 +466,7 @@
             each_way(
                 step, lambda way, lvl: across_moves(step, way, lvl, half, lambda copy: copy.wait_send())
             )
+    mate_moves(lambda copy: copy.wait_send())
     for r, swap in enumerate(swaps):
         swap.wait()
         band = slice(r * B, (r + 1) * B)

time: 78.3 us -> 73 us (0.932)
  Pallas kernels: 75.8 us -> 70.6 us
    pallas_call x1, Pallas kernels: 75.8 us -> 70.6 us  [gather_plan(): pl.pallas_call(flow_kernel, out_shape=jax.ShapeDtypeStruct((order, order)...]
where the time goes in v4:
time: 73 us; the launch traced here: 72.9 us
  Pallas kernels  70.6 us (97%)
  local copies, waits for them, and re-layouts  2.26 us (3%)
    pallas_call x1, Pallas kernels, gather_plan(): pl.pallas_call(flow_kernel, out_shape=jax.ShapeDtypeStruct((order, order)...  70.6 us
    unnamed x1, local copies, waits for them, and re-layouts  2.26 us

profile of v4, /device:TPU:0, one launch (start us, length us, event | category | flops | bytes accessed | tf_op | source)
XLA Modules:
  0.0 72.9 jit_solution(3432739816976621731)
XLA Ops:
  0.0 70.6 %shard_map.64 = f32[512,512]{1,0:T(8,128)} custom-call(bf16[512,512]{1,0:T(8,128)(2,1)} %eta_hbm.1, bf16[512,512]{1,0:T(8,128)(2,1)} %ham_hbm.1, s32[2,512]{1,0:T(2,128)} %bitcast.8, s32[2,512]{1,0:T(2,128)} %bitcast.9, s32[8,16]{1,0:T(8,128)} %bitcast.10, f32[8,16]{1,0:T(8,128)} %bitcast.11), custom_call_target="tpu_custom_call" | custom-call | tf_op jit(solution)/shard_map/pallas_call | solution.py:482
  70.6 2.3 %copy.8 = f32[512,512]{1,0:T(8,128)} copy(f32[512,512]{1,0:T(8,128)} %shard_map.64) | data formatting | bytes 2097152

commit v5 on v4

--- a/solution.py
+++ b/solution.py
@@ -388,7 +388,7 @@
     for load in loads:
         load.wait()
 
-    part_rows = B // 2
+    part_rows = B
     order = NBR * B
 
     @pl.loop(0, local_count)
@@ -397,7 +397,7 @@
         def _(r):
             for s in range(NBR):
                 scale = packed[2 * q + core, 0, PER_HALF * B :, :][4 + s : 5 + s, :]
-                for part in range(2):
+                for part in range(1):
                     span = pl.ds(part * part_rows, part_rows)
                     total_eta = jnp.zeros((part_rows, B), jnp.float32)
                     total_ham = jnp.zeros((part_rows, B), jnp.float32)
@@ -431,7 +431,7 @@
 
     def sum_back(first, target, r, keep):
         for s in range(NBR):
-            for part in range(2):
+            for part in range(1):
                 span = pl.ds(part * part_rows, part_rows)
                 total = jnp.zeros((part_rows, B), jnp.float32)
                 for q in range(local_count):

time: 73 us -> 72.2 us (0.989)
  Pallas kernels: 70.6 us -> 69.7 us
    pallas_call x1, Pallas kernels: 70.6 us -> 69.7 us  [gather_plan(): pl.pallas_call(flow_kernel, out_shape=jax.ShapeDtypeStruct((order, order)...]
where the time goes in v5:
time: 72.2 us; the launch traced here: 72 us
  Pallas kernels  69.7 us (97%)
  local copies, waits for them, and re-layouts  2.26 us (3%)
    pallas_call x1, Pallas kernels, gather_plan(): pl.pallas_call(flow_kernel, out_shape=jax.ShapeDtypeStruct((order, order)...  69.7 us
    unnamed x1, local copies, waits for them, and re-layouts  2.26 us

profile of v5, /device:TPU:0, one launch (start us, length us, event | category | flops | bytes accessed | tf_op | source)
XLA Modules:
  0.0 72.0 jit_solution(9742488248032451751)
XLA Ops:
  0.0 69.7 %shard_map.64 = f32[512,512]{1,0:T(8,128)} custom-call(bf16[512,512]{1,0:T(8,128)(2,1)} %eta_hbm.1, bf16[512,512]{1,0:T(8,128)(2,1)} %ham_hbm.1, s32[2,512]{1,0:T(2,128)} %bitcast.8, s32[2,512]{1,0:T(2,128)} %bitcast.9, s32[8,16]{1,0:T(8,128)} %bitcast.10, f32[8,16]{1,0:T(8,128)} %bitcast.11), custom_call_target="tpu_custom_call" | custom-call | tf_op jit(solution)/shard_map/pallas_call | solution.py:482
  69.8 2.3 %copy.8 = f32[512,512]{1,0:T(8,128)} copy(f32[512,512]{1,0:T(8,128)} %shard_map.64) | data formatting | bytes 2097152
